TPU v7x, 512 devices: a whole 4x4x16 slice. The times are simulated.
512 devices in a mesh: row: 16 (over z), col: 8 (over x, core), leaf: 4 (over y).
Axes of the slice: x: 4, y: 4, z: 16, core: 2. Of those that a mesh axis runs over, the one named last changes fastest.
Arguments:
- leaf_rhs: bfloat16 [4, 2, 512, 4096], P('leaf', None, 'col', 'row'), may hold values from -6 to 6
- root_rhs: bfloat16 [2, 512, 4096], P(None, 'col', 'row'), may hold values from -6 to 6
- leaf_lower: bfloat16 [4, 1, 4096, 4096], P('leaf', None, 'row', 'col'), may hold values from -0.046875 to 0.046875
- leaf_coupling_lower: bfloat16 [4, 2, 2, 4096, 4096], P('leaf', None, None, 'row', 'col'), may hold values from -0.046875 to 0.046875
- root_lower: bfloat16 [1, 4096, 4096], P(None, 'row', 'col'), may hold values from -0.046875 to 0.046875
- leaf_upper: bfloat16 [4, 1, 4096, 4096], P('leaf', None, 'row', 'col'), may hold values from -0.046875 to 0.046875
- leaf_coupling_upper: bfloat16 [4, 2, 2, 4096, 4096], P('leaf', None, None, 'row', 'col'), may hold values from -0.046875 to 0.046875
- root_upper: bfloat16 [1, 4096, 4096], P(None, 'row', 'col'), may hold values from -0.046875 to 0.046875
- leaf_lower_inv: float32 [4, 2, 32, 128, 128], P('leaf', None, 'row'), may hold values from -1 to 2, as said below
- root_lower_inv: float32 [2, 32, 128, 128], P(None, 'row'), may hold values from -1 to 2, as said below
- leaf_upper_inv: float32 [4, 2, 32, 128, 128], P('leaf', None, 'row'), may hold values from -1 to 2, as said below
- root_upper_inv: float32 [2, 32, 128, 128], P(None, 'row'), may hold values from -1 to 2, as said below
Outputs:
- leaf_solution: bfloat16 [4, 2, 512, 4096], P('leaf', None, 'col', 'row')
- root_solution: bfloat16 [2, 512, 4096], P(None, 'col', 'row')
Inputs may be any that keep to these rules, and one draw needn't show every extreme that they name: `leaf_lower_inv`: each 128 x 128 matrix is lower triangular with unit diagonal. `root_lower_inv`: each 128 x 128 matrix is lower triangular with unit diagonal. `leaf_upper_inv`: each 128 x 128 matrix is upper triangular with a positive diagonal. `root_upper_inv`: each 128 x 128 matrix is upper triangular with a positive diagonal.
All inputs are finite; a program needn't handle non-finite values.
Results may differ from a plain program's by a relative error of at most 0.03.
Values may be sent and summed in bfloat16 or wider, within the bound.
A program may use at most 64 MiB of HBM per device.

v0:
```python
import jax
import jax.numpy as jnp
from jax import lax
from jax.sharding import PartitionSpec as P


def from_root(block, axis, holder):
    block = jnp.where(lax.axis_index(axis) == holder, block, jnp.zeros_like(block))
    return lax.psum(block, axis)


def pair_index(high, low):
    return high * (high - 1) // 2 + low


def multiply(pieces, block):
    return lax.dot_general(
        pieces, block, (((1,), (1,)), ((), ())), preferred_element_type=jnp.float32
    )


def invert(inverse, right_side):
    rhs_count = right_side.shape[0]
    blocks = inverse.shape[0]
    block_width = inverse.shape[1]
    blocked = right_side.reshape(rhs_count, blocks, block_width)
    result = jnp.einsum("sab,qsb->qsa", inverse, blocked, precision=lax.Precision.HIGHEST)
    return result.reshape(rhs_count, blocks * block_width).astype(jnp.bfloat16)


def spread(gathered):
    column = lax.axis_index("col")
    group = lax.axis_size("row") // lax.axis_size("col")
    pieces = []
    for offset in range(group):
        pieces.append(from_root(gathered, "row", column * group + offset))
    return jnp.concatenate(pieces, axis=1)


def settle(products, own_part, inverse, needed):
    gathered = None
    right_side = own_part.astype(jnp.float32)
    if products is not None:
        right_side = right_side - lax.psum_scatter(
            products.astype(jnp.bfloat16), "col", scatter_dimension=0, tiled=True
        ).astype(jnp.float32)
    solved = invert(inverse, right_side)
    if needed:
        gathered = lax.all_gather(solved, "col", axis=0, tiled=True)
    return (solved, gathered)


def accumulate(products, partial_value):
    if products is None:
        return partial_value
    return products + partial_value


def on_device(
    leaf_rhs,
    root_rhs,
    leaf_lower,
    leaf_coupling_lower,
    root_lower,
    leaf_upper,
    leaf_coupling_upper,
    root_upper,
    leaf_lower_inv,
    root_lower_inv,
    leaf_upper_inv,
    root_upper_inv,
):
    leaf_levels = leaf_rhs.shape[1]
    root_levels = root_rhs.shape[0]
    leaf_share = []
    leaf_columns = []
    for k in range(leaf_levels):
        products = None
        for j in range(k):
            products = accumulate(
                products, multiply(leaf_columns[j], leaf_lower[0, pair_index(k, j)])
            )
        solved, gathered = settle(products, leaf_rhs[0, k], leaf_lower_inv[0, k], True)
        leaf_share.append(solved)
        leaf_columns.append(spread(gathered))
    coupling = []
    for m in range(root_levels):
        products = None
        for j in range(leaf_levels):
            products = accumulate(products, multiply(leaf_columns[j], leaf_coupling_lower[0, m, j]))
        coupling.append(products)
    summed = lax.psum(jnp.stack(coupling).astype(jnp.bfloat16), "leaf").astype(jnp.float32)
    root_share = []
    root_columns = []
    for m in range(root_levels):
        products = summed[m]
        for i in range(m):
            products = products + multiply(root_columns[i], root_lower[pair_index(m, i)])
        needed = m + 1 < root_levels
        solved, gathered = settle(products, root_rhs[m], root_lower_inv[m], needed)
        root_share.append(solved)
        root_columns.append(spread(gathered) if needed else None)
    root_back = [None] * root_levels
    root_out = [None] * root_levels
    for m in reversed(range(root_levels)):
        products = None
        for i in range(m + 1, root_levels):
            products = accumulate(products, multiply(root_back[i], root_upper[pair_index(i, m)]))
        solved, gathered = settle(products, root_share[m], root_upper_inv[m], True)
        root_back[m] = spread(gathered)
        root_out[m] = solved
    leaf_back = [None] * leaf_levels
    leaf_out = [None] * leaf_levels
    for k in reversed(range(leaf_levels)):
        products = None
        for j in range(k + 1, leaf_levels):
            products = accumulate(products, multiply(leaf_back[j], leaf_upper[0, pair_index(j, k)]))
        for m in range(root_levels):
            products = accumulate(products, multiply(root_back[m], leaf_coupling_upper[0, k, m]))
        solved, gathered = settle(products, leaf_share[k], leaf_upper_inv[0, k], k > 0)
        leaf_out[k] = solved
        if k > 0:
            leaf_back[k] = spread(gathered)
    return (jnp.stack(leaf_out)[None], jnp.stack(root_out))


def solution(mesh):
    placed = (
        P("leaf", None, "col", "row"),
        P(None, "col", "row"),
        P("leaf", None, "row", "col"),
        P("leaf", None, None, "row", "col"),
        P(None, "row", "col"),
        P("leaf", None, "row", "col"),
        P("leaf", None, None, "row", "col"),
        P(None, "row", "col"),
        P("leaf", None, "row", None, None),
        P(None, "row", None, None),
        P("leaf", None, "row", None, None),
        P(None, "row", None, None),
    )
    return jax.shard_map(
        on_device,
        mesh=mesh,
        in_specs=placed,
        out_specs=(P("leaf", None, "col", "row"), P(None, "col", "row")),
        check_vma=False,
    )
```

profile of v0, /device:TPU:1, one launch (start us, length us, event | category | flops | bytes accessed | tf_op | source)
XLA Modules:
  0.0 1220.8 jit_solution(11090391771171426800)
XLA Ops:
  7.2 0.8 slice-done
  8.0 1.1 fusion.7
  9.2 19.6 %all_gather.18 = bf16[512,256]{1,0:T(8,128)(2,1)S(1)} all-gather(bf16[64,256]{1,0:T(8,128)(2,1)S(1)} %bitcast.198), channel_id=1, replica_groups=mesh['row'=16,'col'=8,'leaf'=4] {'col'}, dimensions={0}, use_global_device_ids=true | all-gather | bytes 294912 | tf_op jit(solution)/shard_map/all_gather | solution.py:49
  28.7 0.8 broadcast_select_fusion.5
  29.7 126.0 %all-reduce.26.cloned.1.call-done = (bf16[512,256]{1,0:T(8,128)(2,1)}, bf16[512,256]{1,0:T(8,128)(2,1)}) async-done(((bf16[512,256]{1,0:T(8,128)(2,1)}, bf16[512,256]{1,0:T(8,128)(2,1)}), (bf16[512,256]{1,0:T(8,128)(2,1)}, bf16[512,256]{1,0:T(8,128)(2,1)})) %all-reduce.26.cloned.1.call-update) | async-done | bytes 524304 | tf_op jit(solution)/shard_map/psum | solution.py:9
  155.6 1.0 constant_dynamic-update-slice_fusion.1
  156.7 1.0 convolution_convert_fusion.1
  157.7 0.0 all-reduce.24.cloned.1.call-start
  157.8 43.7 %reduce-scatter.7.cloned.1.call-done = bf16[64,256]{1,0:T(8,128)(2,1)} async-done(((bf16[512,256]{1,0:T(8,128)(2,1)}), bf16[64,256]{1,0:T(8,128)(2,1)}) %reduce-scatter.7.cloned.1.call-update) | async-done | bytes 32784 | tf_op jit(solution)/shard_map/reduce_scatter | solution.py:44
  201.5 1.1 fusion.8
  202.6 14.9 %all_gather.19 = bf16[512,256]{1,0:T(8,128)(2,1)S(1)} all-gather(bf16[64,256]{1,0:T(8,128)(2,1)S(1)} %bitcast.199), channel_id=1, replica_groups=mesh['row'=16,'col'=8,'leaf'=4] {'col'}, dimensions={0}, use_global_device_ids=true | all-gather | bytes 294912 | tf_op jit(solution)/shard_map/all_gather | solution.py:49
  217.5 0.8 broadcast_select_fusion.4
  218.5 0.3 fusion.28
  218.8 0.3 fusion.31
  219.1 126.3 %all-reduce.24.cloned.1.call-done = (bf16[512,256]{1,0:T(8,128)(2,1)}, bf16[512,256]{1,0:T(8,128)(2,1)}) async-done(((bf16[512,256]{1,0:T(8,128)(2,1)}, bf16[512,256]{1,0:T(8,128)(2,1)}), (bf16[512,256]{1,0:T(8,128)(2,1)}, bf16[512,256]{1,0:T(8,128)(2,1)})) %all-reduce.24.cloned.1.call-update) | async-done | bytes 524304 | tf_op jit(solution)/shard_map/psum | solution.py:9
  345.4 1.0 constant_dynamic-update-slice_fusion.3
  346.5 0.3 fusion.5
  346.8 0.3 fusion.6
  347.1 0.9 pad_maximum_fusion
  348.0 0.0 reduce-scatter.9.cloned.1.call-start
  348.1 62.7 %all-reduce.14.cloned.1.call-done = bf16[2,512,256]{2,1,0:T(8,128)(2,1)} async-done(((bf16[2,512,256]{2,1,0:T(8,128)(2,1)}), bf16[2,512,256]{2,1,0:T(8,128)(2,1)}) %all-reduce.14.cloned.1.call-update) | async-done | bytes 524304 | tf_op jit(solution)/shard_map/psum | solution.py:92
  410.7 1.7 slice_bitcast_fusion.1
  412.5 40.6 %reduce-scatter.9.cloned.1.call-done = bf16[64,256]{1,0:T(8,128)(2,1)} async-done(((bf16[512,256]{1,0:T(8,128)(2,1)}), bf16[64,256]{1,0:T(8,128)(2,1)}) %reduce-scatter.9.cloned.1.call-update) | async-done | bytes 32784 | tf_op jit(solution)/shard_map/reduce_scatter | solution.py:44
  453.0 1.1 fusion.9
  454.2 14.9 %all_gather.20 = bf16[512,256]{1,0:T(8,128)(2,1)S(1)} all-gather(bf16[64,256]{1,0:T(8,128)(2,1)S(1)} %bitcast.200), channel_id=1, replica_groups=mesh['row'=16,'col'=8,'leaf'=4] {'col'}, dimensions={0}, use_global_device_ids=true | all-gather | bytes 294912 | tf_op jit(solution)/shard_map/all_gather | solution.py:49
  469.1 0.8 broadcast_select_fusion.9
  469.9 0.0 reduce-scatter.11.cloned.1.call-start
  470.0 126.9 %all-reduce.22.cloned.1.call-done = (bf16[512,256]{1,0:T(8,128)(2,1)}, bf16[512,256]{1,0:T(8,128)(2,1)}) async-done(((bf16[512,256]{1,0:T(8,128)(2,1)}, bf16[512,256]{1,0:T(8,128)(2,1)}), (bf16[512,256]{1,0:T(8,128)(2,1)}, bf16[512,256]{1,0:T(8,128)(2,1)})) %all-reduce.22.cloned.1.call-update) | async-done | bytes 524304 | tf_op jit(solution)/shard_map/psum | solution.py:9
  596.9 2.0 fusion.2
  599.0 0.0 all-reduce.20.cloned.1.call-start
  599.0 43.8 %reduce-scatter.11.cloned.1.call-done = bf16[64,256]{1,0:T(8,128)(2,1)} async-done(((bf16[512,256]{1,0:T(8,128)(2,1)}), bf16[64,256]{1,0:T(8,128)(2,1)}) %reduce-scatter.11.cloned.1.call-update) | async-done | bytes 32784 | tf_op jit(solution)/shard_map/reduce_scatter | solution.py:44
  642.8 1.1 fusion.10
  643.9 0.2 convolution_convert_fusion.5
  644.2 14.9 %all_gather.21 = bf16[512,256]{1,0:T(8,128)(2,1)S(1)} all-gather(bf16[64,256]{1,0:T(8,128)(2,1)S(1)} %copy_bitcast_fusion.2), channel_id=1, replica_groups=mesh['row'=16,'col'=8,'leaf'=4] {'col'}, dimensions={0}, use_global_device_ids=true | all-gather | bytes 294912 | tf_op jit(solution)/shard_map/all_gather | solution.py:49
  659.1 0.8 broadcast_select_fusion.2
  659.9 0.0 reduce-scatter.13.cloned.1.call-start
  660.0 126.9 %all-reduce.20.cloned.1.call-done = (bf16[512,256]{1,0:T(8,128)(2,1)}, bf16[512,256]{1,0:T(8,128)(2,1)}) async-done(((bf16[512,256]{1,0:T(8,128)(2,1)}, bf16[512,256]{1,0:T(8,128)(2,1)}), (bf16[512,256]{1,0:T(8,128)(2,1)}, bf16[512,256]{1,0:T(8,128)(2,1)})) %all-reduce.20.cloned.1.call-update) | async-done | bytes 524304 | tf_op jit(solution)/shard_map/psum | solution.py:9
  786.9 1.0 constant_dynamic-update-slice_fusion.5
  788.0 0.9 copy-done.11
  788.9 1.0 convolution_convert_fusion
  789.9 0.0 all-reduce.18.cloned.1.call-start
  790.0 43.0 %reduce-scatter.13.cloned.1.call-done = bf16[64,256]{1,0:T(8,128)(2,1)} async-done(((bf16[512,256]{1,0:T(8,128)(2,1)}), bf16[64,256]{1,0:T(8,128)(2,1)}) %reduce-scatter.13.cloned.1.call-update) | async-done | bytes 32784 | tf_op jit(solution)/shard_map/reduce_scatter | solution.py:44
  832.9 1.1 convolution_convert_fusion.4
  834.1 14.9 %all_gather.22 = bf16[512,256]{1,0:T(8,128)(2,1)S(1)} all-gather(bf16[64,256]{1,0:T(8,128)(2,1)S(1)} %copy_bitcast_fusion.1), channel_id=1, replica_groups=mesh['row'=16,'col'=8,'leaf'=4] {'col'}, dimensions={0}, use_global_device_ids=true | all-gather | bytes 294912 | tf_op jit(solution)/shard_map/all_gather | solution.py:49
  849.0 0.8 broadcast_select_fusion.1
  849.8 0.0 reduce-scatter.15.cloned.1.call-start
  849.9 126.9 %all-reduce.18.cloned.1.call-done = (bf16[512,256]{1,0:T(8,128)(2,1)}, bf16[512,256]{1,0:T(8,128)(2,1)}) async-done(((bf16[512,256]{1,0:T(8,128)(2,1)}, bf16[512,256]{1,0:T(8,128)(2,1)}), (bf16[512,256]{1,0:T(8,128)(2,1)}, bf16[512,256]{1,0:T(8,128)(2,1)})) %all-reduce.18.cloned.1.call-update) | async-done | bytes 524304 | tf_op jit(solution)/shard_map/psum | solution.py:9
  976.8 1.0 constant_dynamic-update-slice_fusion.7
  977.8 0.3 fusion.23
  978.2 1.0 fusion.3
  979.2 0.0 all-reduce.16.cloned.1.call-start
  979.3 43.4 %reduce-scatter.15.cloned.1.call-done = bf16[64,256]{1,0:T(8,128)(2,1)} async-done(((bf16[512,256]{1,0:T(8,128)(2,1)}), bf16[64,256]{1,0:T(8,128)(2,1)}) %reduce-scatter.15.cloned.1.call-update) | async-done | bytes 32784 | tf_op jit(solution)/shard_map/reduce_scatter | solution.py:44
  1022.7 1.1 convolution_convert_fusion.3
  1023.8 14.9 %all_gather.23 = bf16[512,256]{1,0:T(8,128)(2,1)S(1)} all-gather(bf16[64,256]{1,0:T(8,128)(2,1)S(1)} %copy_bitcast_fusion), channel_id=1, replica_groups=mesh['row'=16,'col'=8,'leaf'=4] {'col'}, dimensions={0}, use_global_device_ids=true | all-gather | bytes 294912 | tf_op jit(solution)/shard_map/all_gather | solution.py:49
  1038.7 0.8 broadcast_select_fusion.6
  1039.6 0.0 reduce-scatter.17.cloned.1.call-start
  1039.6 126.9 %all-reduce.16.cloned.1.call-done = (bf16[512,256]{1,0:T(8,128)(2,1)}, bf16[512,256]{1,0:T(8,128)(2,1)}) async-done(((bf16[512,256]{1,0:T(8,128)(2,1)}, bf16[512,256]{1,0:T(8,128)(2,1)}), (bf16[512,256]{1,0:T(8,128)(2,1)}, bf16[512,256]{1,0:T(8,128)(2,1)})) %all-reduce.16.cloned.1.call-update) | async-done | bytes 524304 | tf_op jit(solution)/shard_map/psum | solution.py:9
  1166.6 1.4 fusion.15
  1167.9 0.3 convolution_add_fusion.1
  1168.3 1.0 fusion.4
  1169.5 0.6 pad_maximum_fusion.1
  1170.2 42.3 %reduce-scatter.17.cloned.1.call-done = bf16[64,256]{1,0:T(8,128)(2,1)} async-done(((bf16[512,256]{1,0:T(8,128)(2,1)}), bf16[64,256]{1,0:T(8,128)(2,1)}) %reduce-scatter.17.cloned.1.call-update) | async-done | bytes 32784 | tf_op jit(solution)/shard_map/reduce_scatter | solution.py:44
  1212.5 1.1 fusion.11
  1213.7 0.6 maximum_bitcast_fusion
  (70 shorter events, 0.9 us)
Async XLA Ops:
  7.2 149.5 %copy-start = (bf16[1,1,256,512]{3,2,1,0:T(8,128)(2,1)S(1)}, bf16[1,1,256,512]{3,2,1,0:T(8,128)(2,1)}, u32[]{:S(2)}) copy-start(bf16[1,1,256,512]{3,2,1,0:T(8,128)(2,1)} %param.14) | copy-start | bytes 786436
  7.2 148.4 %all-reduce.26.cloned.1.call-start = ((), (), s32[]{:S(2)}) async-start(), calls=%async_computation.18 | async-start | bytes 1048576 | tf_op jit(solution)/shard_map/psum | solution.py:9
  7.2 0.8 slice-start
  29.6 171.9 %reduce-scatter.7.cloned.1.call-start = ((), (), s32[]{:S(2)}) async-start(), calls=%async_computation.6 | async-start | bytes 294912 | tf_op jit(solution)/shard_map/reduce_scatter | solution.py:44
  155.6 1.0 copy-start.8
  156.7 44.8 %copy-start.13 = (bf16[1,2,64,256]{3,2,1,0:T(8,128)(2,1)S(1)}, bf16[1,2,64,256]{3,2,1,0:T(8,128)(2,1)}, u32[]{:S(2)}) copy-start(bf16[1,2,64,256]{3,2,1,0:T(8,128)(2,1)} %param.12) | copy-start | bytes 196612
  157.7 43.8 %copy-start.3 = (f32[1,2,2,128,128]{4,3,2,1,0:T(8,128)S(1)}, f32[1,2,2,128,128]{4,3,2,1,0:T(8,128)}, u32[]{:S(2)}) copy-start(f32[1,2,2,128,128]{4,3,2,1,0:T(8,128)} %param.20) | copy-start | bytes 786436
  157.7 60.8 %copy-start.1 = (bf16[1,2,2,256,512]{4,3,2,1,0:T(8,128)(2,1)S(1)}, bf16[1,2,2,256,512]{4,3,2,1,0:T(8,128)(2,1)}, u32[]{:S(2)}) copy-start(bf16[1,2,2,256,512]{4,3,2,1,0:T(8,128)(2,1)} %param.15) | copy-start | bytes 3145732
  157.7 187.7 %all-reduce.24.cloned.1.call-start = ((), (), s32[]{:S(2)}) async-start(), calls=%async_computation.17 | async-start | bytes 1048576 | tf_op jit(solution)/shard_map/psum | solution.py:9
  218.4 192.3 %all-reduce.14.cloned.1.call-start = ((), (), s32[]{:S(2)}) async-start(), calls=%async_computation.7 | async-start | bytes 1048576 | tf_op jit(solution)/shard_map/psum | solution.py:92
  345.4 1.0 copy-start.7
  348.0 105.0 %reduce-scatter.9.cloned.1.call-start = ((), (), s32[]{:S(2)}) async-start(), calls=%async_computation.8 | async-start | bytes 294912 | tf_op jit(solution)/shard_map/reduce_scatter | solution.py:44
  410.7 42.3 %copy-start.14 = (bf16[2,64,256]{2,1,0:T(8,128)(2,1)S(1)}, bf16[2,64,256]{2,1,0:T(8,128)(2,1)}, u32[]{:S(2)}) copy-start(bf16[2,64,256]{2,1,0:T(8,128)(2,1)} %param.13) | copy-start | bytes 196612
  412.4 40.6 %copy-start.4 = (f32[2,2,128,128]{3,2,1,0:T(8,128)S(1)}, f32[2,2,128,128]{3,2,1,0:T(8,128)}, u32[]{:S(2)}) copy-start(f32[2,2,128,128]{3,2,1,0:T(8,128)} %param.21) | copy-start | bytes 786436
  412.4 184.4 %all-reduce.22.cloned.1.call-start = ((), (), s32[]{:S(2)}) async-start(), calls=%async_computation.16 | async-start | bytes 1048576 | tf_op jit(solution)/shard_map/psum | solution.py:9
  469.1 127.8 %copy-start.12 = (bf16[2,512,256]{2,1,0:T(8,128)(2,1)S(1)}, bf16[2,512,256]{2,1,0:T(8,128)(2,1)}, u32[]{:S(2)}) copy-start(bf16[2,512,256]{2,1,0:T(8,128)(2,1)} %all-reduce.14.cloned.1.call-done) | copy-start | bytes 1572868
  469.9 127.0 %copy-start.15 = (bf16[1,256,512]{2,1,0:T(8,128)(2,1)S(1)}, bf16[1,256,512]{2,1,0:T(8,128)(2,1)}, u32[]{:S(2)}) copy-start(bf16[1,256,512]{2,1,0:T(8,128)(2,1)} %param.16) | copy-start | bytes 786436
  469.9 172.8 %reduce-scatter.11.cloned.1.call-start = ((), (), s32[]{:S(2)}) async-start(), calls=%async_computation.9 | async-start | bytes 294912 | tf_op jit(solution)/shard_map/reduce_scatter | solution.py:44
  598.9 45.0 %copy-start.5 = (f32[2,2,128,128]{3,2,1,0:T(8,128)S(1)}, f32[2,2,128,128]{3,2,1,0:T(8,128)}, u32[]{:S(2)}) copy-start(f32[2,2,128,128]{3,2,1,0:T(8,128)} %param.23) | copy-start | bytes 786436
  599.0 187.9 %all-reduce.20.cloned.1.call-start = ((), (), s32[]{:S(2)}) async-start(), calls=%async_computation.15 | async-start | bytes 1048576 | tf_op jit(solution)/shard_map/psum | solution.py:9
  659.9 173.0 %reduce-scatter.13.cloned.1.call-start = ((), (), s32[]{:S(2)}) async-start(), calls=%async_computation.10 | async-start | bytes 294912 | tf_op jit(solution)/shard_map/reduce_scatter | solution.py:44
  786.9 1.0 copy-start.9
  787.9 0.9 copy-start.11
  789.9 186.8 %all-reduce.18.cloned.1.call-start = ((), (), s32[]{:S(2)}) async-start(), calls=%async_computation.14 | async-start | bytes 1048576 | tf_op jit(solution)/shard_map/psum | solution.py:9
  849.0 128.9 %copy-start.2 = (bf16[1,2,2,256,512]{4,3,2,1,0:T(8,128)(2,1)S(1)}, bf16[1,2,2,256,512]{4,3,2,1,0:T(8,128)(2,1)}, u32[]{:S(2)}) copy-start(bf16[1,2,2,256,512]{4,3,2,1,0:T(8,128)(2,1)} %param.18) | copy-start | bytes 3145732
  849.8 172.8 %reduce-scatter.15.cloned.1.call-start = ((), (), s32[]{:S(2)}) async-start(), calls=%async_computation.11 | async-start | bytes 294912 | tf_op jit(solution)/shard_map/reduce_scatter | solution.py:44
  976.8 1.0 copy-start.10
  979.2 43.5 %copy-start.6 = (f32[1,2,2,128,128]{4,3,2,1,0:T(8,128)S(1)}, f32[1,2,2,128,128]{4,3,2,1,0:T(8,128)}, u32[]{:S(2)}) copy-start(f32[1,2,2,128,128]{4,3,2,1,0:T(8,128)} %param.22) | copy-start | bytes 786436
  979.2 187.4 %all-reduce.16.cloned.1.call-start = ((), (), s32[]{:S(2)}) async-start(), calls=%async_computation.13 | async-start | bytes 1048576 | tf_op jit(solution)/shard_map/psum | solution.py:9
  1039.6 127.0 %copy-start.16 = (bf16[1,1,256,512]{3,2,1,0:T(8,128)(2,1)S(1)}, bf16[1,1,256,512]{3,2,1,0:T(8,128)(2,1)}, u32[]{:S(2)}) copy-start(bf16[1,1,256,512]{3,2,1,0:T(8,128)(2,1)} %param.17) | copy-start | bytes 786436
  1039.6 172.9 %reduce-scatter.17.cloned.1.call-start = ((), (), s32[]{:S(2)}) async-start(), calls=%async_computation.12 | async-start | bytes 294912 | tf_op jit(solution)/shard_map/reduce_scatter | solution.py:44
Sparse Core Ops, SparseCore 0:
  29.7 125.8 all-reduce.25
  158.6 42.8 reduce-scatter.6
  218.5 126.8 all-reduce.23
  348.1 62.5 all-reduce.13
  413.6 39.4 reduce-scatter.8
  470.0 126.7 all-reduce.21
  599.9 42.8 reduce-scatter.10
  660.0 126.8 all-reduce.19
  790.0 42.8 reduce-scatter.12
  850.0 126.7 all-reduce.17
  979.8 42.8 reduce-scatter.14
  1039.7 126.8 all-reduce.15
  1169.6 42.8 reduce-scatter.16
where the time goes:
time: 1220 us
  waiting for transfers between devices  1080 us (89%)
  blocking collectives  94 us (8%)
  matrix products  17.5 us (1%)
  between operations  14.3 us (1%)
    psum x6, waiting for transfers between devices, from_root(): return lax.psum(block, axis)  760 us
    reduce_scatter x6, waiting for transfers between devices, settle(): lax.psum_scatter(products.astype(jnp.bfloat16), 'col', scatter_dimension=...  257 us
    all_gather x6, blocking collectives, settle(): gathered = lax.all_gather(solved, 'col', axis=0, tiled=True)  94 us
    psum x1, waiting for transfers between devices, on_device(): lax.psum(jnp.stack(coupling).astype(jnp.bfloat16), 'leaf')  62.7 us
  transfers between devices with their start and end apart: 13, of which 13 were waited for; matrix products, arithmetic and copies ran while one was open for 0% of the time, Pallas kernels for 0%

commit v1 on v0

v1 whole, which is shorter than its diff:
```python
import jax
import jax.numpy as jnp
from jax import lax
from jax.experimental import pallas as pl
from jax.experimental.pallas import tpu as pltpu
from jax.sharding import PartitionSpec as P

MESH = pl.DeviceIdType.MESH
H = 2
LH = 4 // H
R = 64 // H
BF = jnp.bfloat16
F32 = jnp.float32
NEAR = [(2, 0), (2, 1), (1, 0), (1, 1), (3, 0), (3, 1), (0, 1)]
N_SEM = 256


def dot_t(a, b):
    return lax.dot_general(a, b, (((1,), (1,)), ((), ())), preferred_element_type=F32)


def solve(inverse, right):
    parts = []
    for s in range(2):
        parts.append(
            lax.dot_general(
                right[:, 128 * s : 128 * (s + 1)],
                inverse[s],
                (((1,), (1,)), ((), ())),
                preferred_element_type=F32,
                precision=lax.Precision.HIGHEST,
            )
        )
    return jnp.concatenate(parts, axis=1).astype(BF)


def kernel(
    leaf_rhs,
    root_rhs,
    leaf_lower,
    coupling_lower,
    root_lower,
    leaf_upper,
    coupling_upper,
    root_upper,
    leaf_lower_inv,
    root_lower_inv,
    leaf_upper_inv,
    root_upper_inv,
    leaf_out,
    root_out,
    b_leaf,
    b_root,
    w_ll,
    w_cl,
    w_rl,
    w_lu,
    w_cu,
    w_ru,
    i_ll,
    i_rl,
    i_lu,
    i_ru,
    yb,
    wb,
    zb,
    xb,
    base1,
    v_y,
    v_w,
    v_z,
    v_x,
    p_y,
    p_a,
    p_w,
    p_r,
    s_y,
    s_a,
    s_w,
    s_r,
    r_y,
    r_a,
    r_w,
    r_r,
    ro,
    sems,
):
    z = lax.axis_index("row")
    c = lax.axis_index("col")
    l = lax.axis_index("leaf")
    x = lax.div(c, 2)
    core = lax.rem(c, 2)
    ct = lax.div(z, 2)
    hl = lax.div(l, LH)
    lt = pl.multiple_of(lax.rem(l, LH) * 16, 16)
    taken = [0]

    def sem():
        taken[0] += 1
        return sems.at[taken[0] - 1]

    def zed(d):
        return lax.rem(z + (d + 32), 16)

    def plane(d):
        return lax.rem(l + (d + 8), 4)

    def colm(dx, dc):
        return lax.rem(x + (dx + 4), 4) * 2 + lax.rem(core + dc, 2)

    def await_bytes(ref, s):
        pltpu.make_async_copy(ref, ref, s).wait()

    sent = []

    def send(src, dst, send_sem, recv_sem, where):
        copy = pltpu.make_async_remote_copy(
            src_ref=src, dst_ref=dst, send_sem=send_sem, recv_sem=recv_sem, device_id=where, device_id_type=MESH
        )
        copy.start()
        return copy

    def load(pairs):
        copies = []
        for src, dst in pairs:
            copy = pltpu.make_async_copy(src, dst, sem())
            copy.start()
            copies.append(copy)

        def done():
            for copy in copies:
                copy.wait()

        return done

    def halves(src, dst):
        return [(src.at[:, pl.ds(256 * b, 256)], dst.at[b]) for b in range(2)]

    first_load = load([(leaf_rhs.at[0], b_leaf), (leaf_lower_inv.at[0], i_ll)])
    load_ll = load(halves(leaf_lower.at[0, 0], w_ll))
    pairs = [(root_rhs, b_root), (root_lower_inv, i_rl), (leaf_upper_inv.at[0], i_lu), (root_upper_inv, i_ru)]
    for m in range(2):
        for j in range(2):
            pairs += halves(coupling_lower.at[0, m, j], w_cl.at[m, j])
            pairs += halves(coupling_upper.at[0, m, j], w_cu.at[m, j])
    pairs += halves(root_lower.at[0], w_rl)
    pairs += halves(leaf_upper.at[0, 0], w_lu)
    pairs += halves(root_upper.at[0], w_ru)
    load_rest = load(pairs)

    barrier = pltpu.get_barrier_semaphore()

    def greet(where):
        pl.semaphore_signal(barrier, inc=1, device_id=where, device_id_type=MESH)

    greeted = 0
    for b in range(2):
        for k in range(8):
            greet((2 * c + b, k, l))
            greeted += 1
    for dy in range(4):
        for dx, dc in NEAR + [(0, 0)]:
            if (dy, dx, dc) != (0, 0, 0):
                greet((z, colm(dx, dc), plane(dy)))
                greeted += 1
    for d in (-2, -1, 1):
        greet((zed(d), c, l))
        greeted += 1

    p_y[...] = jnp.zeros_like(p_y)
    p_a[...] = jnp.zeros_like(p_a)
    p_w[...] = jnp.zeros_like(p_w)

    def spread_far(src, v):
        s_one, s_rest, r = sem(), sem(), sem()
        kind = 2 * lax.rem(z, 2) + lax.div(c, 4)
        off = lax.rem(kind - z + 16, 4)
        dst = v.at[lax.rem(z, 2), c]
        for i in (2, 1, 3):
            send(src, dst, s_rest, r, (zed(off + 4 * i), ct, l))
        first = zed(off)
        me = (first == z) & (ct == c)

        @pl.when(me)
        def _():
            pltpu.make_async_copy(src, dst, r).start()

        @pl.when(jnp.logical_not(me))
        def _():
            send(src, dst, s_one, r, (first, ct, l))

        def finish():
            await_bytes(v.at[0, pl.ds(0, 3)], s_rest)

            @pl.when(jnp.logical_not(me))
            def _():
                await_bytes(src, s_one)

        sent.append(finish)
        return lambda: await_bytes(v.at[0, pl.ds(0, 4)], r)

    def class_of(d):
        j = lax.rem(z + (d + 16), 4)
        return lax.div(j, 2), lax.rem(j, 2) * 4

    def spread_near(v):
        b, first = class_of(0)
        block = v.at[b, pl.ds(first, 4)]
        s = sem()
        waits = []
        for d in (2, 1, -1):
            r = sem()
            send(block, block, s, r, (zed(d), c, l))
            waits.append((-d, r))

        sent.append(lambda: await_bytes(v.at[:, pl.ds(0, 6)], s))

        def arrivals():
            for d, r in (waits[1], waits[2], waits[0]):
                await_bytes(block, r)
                yield d

        return arrivals

    def add_class(acc, v, w, d):
        b, first = class_of(d)
        rows = v[b, pl.ds(first, 4)].reshape(4 * R, 256)
        acc[pl.ds(first, 4)] += dot_t(rows, w[b]).reshape(4, R, 256)

    def add_all(acc, v, w):
        total = dot_t(v[0].reshape(8 * R, 256), w[0]) + dot_t(v[1].reshape(8 * R, 256), w[1])
        acc[...] += total.reshape(8, R, 256)

    def reduce_start(p, s_ref, r_ref):
        s, r = sem(), sem()
        s_ref[...] = p[...].astype(BF)
        for i, (dx, dc) in enumerate(NEAR):
            other = colm(dx, dc)
            send(s_ref.at[other], r_ref.at[i], s, r, (z, other, l))
        sent.append(lambda: await_bytes(r_ref, s))

        def result():
            await_bytes(r_ref, r)
            total = p[c]
            for i in range(7):
                total = total + r_ref[i].astype(F32)
            return total

        return result

    a_recv = [sem(), sem()]

    def reduce_leaf_start(m, h):
        s_ref = s_a.at[m, h]
        s_ref[...] = p_a[m, h].astype(BF)
        s = sem()
        for dx, dc in NEAR + [(0, 0)]:
            for t in range(LH):
                there = h * LH + t
                other = colm(dx, dc)
                k = (NEAR + [(0, 0)]).index((dx, dc))
                slot = lax.rem(l - there + 4, 4)
                src = s_ref.at[other, pl.ds(16 * t, 16)]
                dst = r_a.at[m, 4 * k + slot - (k == 7)]
                if (dx, dc) == (0, 0):
                    own = sem()
                    away = l != there

                    @pl.when(away)
                    def _():
                        send(src, dst, own, a_recv[m], (z, other, there))

                    def finish(away=away, own=own, src=src):
                        @pl.when(away)
                        def _():
                            await_bytes(src, own)

                    sent.append(finish)
                else:
                    send(src, dst, s, a_recv[m], (z, other, there))
        sent.append(lambda: await_bytes(s_ref.at[pl.ds(0, 7)], s))

    def reduce_leaf_result(m):
        await_bytes(r_a.at[m], a_recv[m])
        total = p_a[m, hl, c, pl.ds(lt, 16)]
        for slot in range(31):
            total = total + r_a[m, slot].astype(F32)
        return total

    def spread_root(src, dst):
        s_one, s_rest, r = sem(), sem(), sem()
        for d in (8, 7, 9, 6, 10, 5, 11, 4, 12, 3, 13, 2, 14, 1, 15):
            send(src, dst, s_rest, r, (zed(d), ct, l))
        me = ct == c

        @pl.when(me)
        def _():
            pltpu.make_async_copy(src, dst, r).start()

        @pl.when(jnp.logical_not(me))
        def _():
            send(src, dst, s_one, r, (z, ct, l))

        def finish():
            await_bytes(r_a.at[0, pl.ds(0, 15)], s_rest)

            @pl.when(jnp.logical_not(me))
            def _():
                await_bytes(src, s_one)

        sent.append(finish)
        return lambda: await_bytes(v_z, r)

    def multiply_root(get, w, p):
        total = dot_t(get(0).reshape(128, 256), w[0]) + dot_t(get(1).reshape(128, 256), w[1])
        p[...] = total.reshape(8, 16, 256)

    lower_b = lambda k, h: b_leaf[k, pl.ds(R * h, R)].astype(F32)

    pl.semaphore_wait(barrier, greeted)
    first_load()

    def lower(h):
        yb[0, h] = solve(i_ll.at[0], lower_b(0, h))
        far = spread_far(yb.at[0, h], v_y.at[0, h])
        if h == 0:
            load_ll()
        yield
        far()
        near = spread_near(v_y.at[0, h])
        add_class(p_y.at[h], v_y.at[0, h], w_ll, 0)
        yield
        for d in near():
            add_class(p_y.at[h], v_y.at[0, h], w_ll, d)
        total = reduce_start(p_y.at[h], s_y.at[h], r_y.at[h])
        if h == 0:
            load_rest()
        for m in range(2):
            add_all(p_a.at[m, h], v_y.at[0, h], w_cl.at[m, 0])
        yield
        yb[1, h] = solve(i_ll.at[1], lower_b(1, h) - total())
        far = spread_far(yb.at[1, h], v_y.at[1, h])
        yield
        far()
        near = spread_near(v_y.at[1, h])
        add_class(p_a.at[0, h], v_y.at[1, h], w_cl.at[0, 1], 0)
        yield
        for d in near():
            add_class(p_a.at[0, h], v_y.at[1, h], w_cl.at[0, 1], d)
        reduce_leaf_start(0, h)
        yield
        add_all(p_a.at[1, h], v_y.at[1, h], w_cl.at[1, 1])
        reduce_leaf_start(1, h)

    gathered = {}

    def x_part(m):
        return v_x.at[m, hl, :, :, pl.ds(lt, 16), :]

    def gather_send(m):
        send_sems = [sem() for _ in range(3)]
        first = taken[0]
        taken[0] += 4
        for i, d in enumerate((2, 1, 3)):
            send(x_part(m), x_part(m), send_sems[i], sems.at[first + (4 - d)], (z, c, plane(d)))
            sent.append(lambda s=send_sems[i]: await_bytes(v_z, s))
        gathered[m] = first

    def gather_wait(m, h):
        for t in range(LH):
            there = h * LH + t
            d = lax.rem(there - l + 4, 4)

            @pl.when(d != 0)
            def _():
                await_bytes(v_z, sems.at[gathered[m] + d])

    out_first = {}

    def out_send(m):
        first = taken[0]
        taken[0] += 4
        ro[m, l] = xb[m]
        for d in (2, 1, 3):
            s = sem()
            send(xb.at[m], ro.at[m, l], s, sems.at[first + (4 - d)], (z, c, plane(d)))
            sent.append(lambda s=s: await_bytes(xb.at[m], s))
        out_first[m] = first

    def out_wait(m):
        for d in (1, 2, 3):
            await_bytes(xb.at[m], sems.at[out_first[m] + d])

    def root():
        rows = pl.ds(pl.multiple_of(l * 16, 16), 16)
        zb[0] = solve(i_rl.at[0], b_root[0, rows].astype(F32) - reduce_leaf_result(0))
        done = spread_root(zb.at[0], v_z.at[lax.rem(z, 2), c])
        base1[...] = b_root[1, rows].astype(F32) - reduce_leaf_result(1)
        done()
        multiply_root(lambda b: v_z[b], w_rl, p_r.at[0])
        total = reduce_start(p_r.at[0], s_r.at[0], r_r.at[0])
        z1 = solve(i_rl.at[1], base1[...] - total())
        xb[1] = solve(i_ru.at[1], z1.astype(F32))
        done = spread_root(xb.at[1], v_x.at[1, hl, lax.rem(z, 2), c, pl.ds(lt, 16)])
        out_send(1)
        done()
        gather_send(1)
        multiply_root(lambda b: v_x[1, hl, b, :, pl.ds(lt, 16), :], w_ru, p_r.at[1])
        total = reduce_start(p_r.at[1], s_r.at[1], r_r.at[1])
        xb[0] = solve(i_ru.at[0], zb[0].astype(F32) - total())
        done = spread_root(xb.at[0], v_x.at[0, hl, lax.rem(z, 2), c, pl.ds(lt, 16)])
        out_send(0)
        for h in range(H):
            gather_wait(1, h)
            for k in (1, 0):
                add_all(p_w.at[k, h], v_x.at[1, h], w_cu.at[k, 1])
        done()
        gather_send(0)

    def upper(h):
        gather_wait(0, h)
        add_all(p_w.at[1, h], v_x.at[0, h], w_cu.at[1, 0])
        total = reduce_start(p_w.at[1, h], s_w.at[1, h], r_w.at[1, h])
        add_all(p_w.at[0, h], v_x.at[0, h], w_cu.at[0, 0])
        yield
        wb[h] = solve(i_lu.at[1], yb[1, h].astype(F32) - total())
        far = spread_far(wb.at[h], v_w.at[h])
        leaf_out[0, 1, pl.ds(R * h, R)] = wb[h]
        yield
        far()
        near = spread_near(v_w.at[h])
        add_class(p_w.at[0, h], v_w.at[h], w_lu, 0)
        yield
        for d in near():
            add_class(p_w.at[0, h], v_w.at[h], w_lu, d)
        total = reduce_start(p_w.at[0, h], s_w.at[0, h], r_w.at[0, h])
        yield
        leaf_out[0, 0, pl.ds(R * h, R)] = solve(i_lu.at[0], yb[0, h].astype(F32) - total())

    def in_turn(chains):
        chains = list(chains)
        while chains:
            chains = [chain for chain in chains if next(chain, chain) is not chain]

    in_turn([lower(h) for h in range(H)])
    root()
    in_turn([upper(h) for h in range(H)])
    for m in range(2):
        out_wait(m)
        root_out[m] = ro[m].reshape(64, 256)
    for finish in sent:
        finish()


def on_device(*args):
    vmem = pltpu.VMEM
    scratch = [
        vmem((2, 64, 256), BF),
        vmem((2, 64, 256), BF),
        vmem((2, 256, 256), BF),
        vmem((2, 2, 2, 256, 256), BF),
        vmem((2, 256, 256), BF),
        vmem((2, 256, 256), BF),
        vmem((2, 2, 2, 256, 256), BF),
        vmem((2, 256, 256), BF),
        vmem((2, 2, 128, 128), F32),
        vmem((2, 2, 128, 128), F32),
        vmem((2, 2, 128, 128), F32),
        vmem((2, 2, 128, 128), F32),
        vmem((2, H, R, 256), BF),
        vmem((H, R, 256), BF),
        vmem((2, 16, 256), BF),
        vmem((2, 16, 256), BF),
        vmem((16, 256), F32),
        vmem((2, H, 2, 8, R, 256), BF),
        vmem((H, 2, 8, R, 256), BF),
        vmem((2, 8, 16, 256), BF),
        vmem((2, H, 2, 8, R, 256), BF),
        vmem((H, 8, R, 256), F32),
        vmem((2, H, 8, R, 256), F32),
        vmem((2, H, 8, R, 256), F32),
        vmem((2, 8, 16, 256), F32),
        vmem((H, 8, R, 256), BF),
        vmem((2, H, 8, R, 256), BF),
        vmem((2, H, 8, R, 256), BF),
        vmem((2, 8, 16, 256), BF),
        vmem((H, 7, R, 256), BF),
        vmem((2, 31, 16, 256), BF),
        vmem((2, H, 7, R, 256), BF),
        vmem((2, 7, 16, 256), BF),
        vmem((2, 4, 16, 256), BF),
        pltpu.SemaphoreType.DMA((N_SEM,)),
    ]
    return pl.pallas_call(
        kernel,
        out_shape=(
            jax.ShapeDtypeStruct((1, 2, 64, 256), BF),
            jax.ShapeDtypeStruct((2, 64, 256), BF),
        ),
        in_specs=[pl.BlockSpec(memory_space=pl.ANY)] * 12,
        out_specs=(pl.BlockSpec(memory_space=pltpu.VMEM),) * 2,
        scratch_shapes=scratch,
        compiler_params=pltpu.CompilerParams(
            collective_id=0, has_side_effects=True, vmem_limit_bytes=48 * 2**20
        ),
    )(*args)


def solution(mesh):
    placed = (
        P("leaf", None, "col", "row"),
        P(None, "col", "row"),
        P("leaf", None, "row", "col"),
        P("leaf", None, None, "row", "col"),
        P(None, "row", "col"),
        P("leaf", None, "row", "col"),
        P("leaf", None, None, "row", "col"),
        P(None, "row", "col"),
        P("leaf", None, "row", None, None),
        P(None, "row", None, None),
        P("leaf", None, "row", None, None),
        P(None, "row", None, None),
    )
    return jax.shard_map(
        on_device,
        mesh=mesh,
        in_specs=placed,
        out_specs=(P("leaf", None, "col", "row"), P(None, "col", "row")),
        check_vma=False,
    )
```

time: 1220 us -> 150 us (0.12)
  waiting for transfers between devices: 1080 us -> 0 us
  Pallas kernels: 0 us -> 136 us
  blocking collectives: 94 us -> 0 us
  matrix products: 17.5 us -> 0 us
  between operations: 14.3 us -> 0.66 us
    psum x7 -> x0, waiting for transfers between devices: 823 us -> none  [the longest x6 760 us: from_root(): return lax.psum(block, axis)]
    reduce_scatter x6 -> x0, waiting for transfers between devices: 257 us -> none  [settle(): lax.psum_scatter(products.astype(jnp.bfloat16), 'col', scatter_dimension=...]
    pallas_call x0 -> x1, Pallas kernels: none -> 136 us  [on_device(): pl.pallas_call(kernel, out_shape=(jax.ShapeDtypeStruct((1, 2, 64, 256), B...]
    all_gather x6 -> x0, blocking collectives: 94 us -> none  [settle(): gathered = lax.all_gather(solved, 'col', axis=0, tiled=True)]
    dot_general x20 -> x0, matrix products: 17.5 us -> none  [the longest x12 9.45 us: multiply(): lax.dot_general(pieces, block, (((1,), (1,)), ((), ())), preferred_elemen...]
  transfers between devices with their start and end apart: 13 -> 0, of which waited for: 13 -> 0; matrix products, arithmetic and copies ran while one was open for 0% -> 0% of each run, Pallas kernels for 0% -> 0%
where the time goes in v1:
time: 150 us
  Pallas kernels  136 us (91%)
  local copies, waits for them, and re-layouts  13 us (9%)
    pallas_call x1, Pallas kernels, on_device(): pl.pallas_call(kernel, out_shape=(jax.ShapeDtypeStruct((1, 2, 64, 256), B...  136 us
    unnamed x26, local copies, waits for them, and re-layouts  13 us

profile of v1, /device:TPU:1, one launch (start us, length us, event | category | flops | bytes accessed | tf_op | source)
XLA Modules:
  0.0 149.9 jit_solution(10029705487055748771)
XLA Ops:
  0.6 0.0 copy-start
  0.6 1.2 copy-done
  1.9 0.0 copy-start.1
  1.9 1.2 copy-done.1
  3.1 0.0 copy-start.2
  3.1 0.9 copy-done.2
  4.0 0.0 copy-start.3
  4.0 0.9 copy-done.3
  5.0 0.0 copy-start.4
  5.0 0.9 copy-done.4
  5.9 0.0 copy-start.5
  5.9 0.9 copy-done.5
  6.9 0.0 copy-start.6
  6.9 0.9 copy-done.6
  7.8 0.0 copy-start.7
  7.8 0.9 copy-done.7
  8.8 0.0 copy-start.8
  8.8 0.9 copy-done.8
  9.7 0.0 copy-start.9
  9.7 0.9 copy-done.9
  10.7 0.0 copy-start.10
  10.7 0.8 copy-done.10
  11.5 0.0 copy-start.11
  11.5 0.8 copy-done.11
  12.4 136.3 %shard_map.131 = (bf16[1,2,64,256]{3,2,1,0:T(8,128)(2,1)S(1)}, bf16[2,64,256]{2,1,0:T(8,128)(2,1)S(1)}) custom-call(bf16[1,2,64,256]{3,2,1,0:T(8,128)(2,1)S(1)} %copy-done.10, bf16[2,64,256]{2,1,0:T(8,128)(2,1)S(1)} %copy-done.11, bf16[1,1,256,512]{3,2,1,0:T(8,128)(2,1)S(1)} %copy-done.2, bf16[1,2,2,256,512]{4,3,2,1,0:T(8,128)(2,1)S(1)} %copy-done, ...), custom_call_target="tpu_custom_call" | custom-call | tf_op jit(solution)/shard_map/pallas_call | solution.py:494
  148.6 0.6 copy.16
  149.3 0.6 copy.17
Async XLA Ops:
  0.6 1.2 copy-start
  1.9 1.2 copy-start.1
  3.1 0.9 copy-start.2
  4.0 0.9 copy-start.3
  5.0 0.9 copy-start.4
  5.9 0.9 copy-start.5
  6.9 0.9 copy-start.6
  7.8 0.9 copy-start.7
  8.8 0.9 copy-start.8
  9.7 0.9 copy-start.9
  10.7 0.8 copy-start.10
  11.5 0.8 copy-start.11

commit v2 on v1

v2 whole, which is shorter than its diff:
```python
import jax
import jax.numpy as jnp
from jax import lax
from jax.experimental import pallas as pl
from jax.experimental.pallas import tpu as pltpu
from jax.sharding import PartitionSpec as P

MESH = pl.DeviceIdType.MESH
H = 4
TURNS = (0, 1, 3, 2)
ORDER = (0, 0, 1, 3, 2, 0, 1, 3, 2, 0, 1, 3, 2, 0, 1, 3, 2, 1, 3, 2)
R = 64 // H
BF = jnp.bfloat16
F32 = jnp.float32
NEAR = [(2, 0), (2, 1), (1, 0), (1, 1), (3, 0), (3, 1), (0, 1)]
N_SEM = 88


def dot_t(a, b):
    return lax.dot_general(a, b, (((1,), (1,)), ((), ())), preferred_element_type=F32)


def solve(inverse, right):
    parts = []
    for s in range(2):
        parts.append(
            lax.dot_general(
                right[:, 128 * s : 128 * (s + 1)],
                inverse[s],
                (((1,), (1,)), ((), ())),
                preferred_element_type=F32,
                precision=lax.Precision.HIGHEST,
            )
        )
    return jnp.concatenate(parts, axis=1).astype(BF)


def kernel(
    leaf_rhs,
    root_rhs,
    leaf_lower,
    coupling_lower,
    root_lower,
    leaf_upper,
    coupling_upper,
    root_upper,
    leaf_lower_inv,
    root_lower_inv,
    leaf_upper_inv,
    root_upper_inv,
    leaf_out,
    root_out,
    b_leaf,
    b_root,
    w_ll,
    w_cl,
    w_rl,
    w_lu,
    w_cu,
    w_ru,
    i_ll,
    i_rl,
    i_lu,
    i_ru,
    yb,
    wb,
    zb,
    xb,
    base1,
    v_y,
    v_w,
    v_z,
    v_x,
    p_y,
    p_a,
    p_w,
    p_r,
    s_y,
    s_a,
    s_w,
    s_r,
    r_y,
    r_a,
    r_w,
    r_r,
    ro,
    spare,
    bytes_of,
    sems,
):
    z = lax.axis_index("row")
    c = lax.axis_index("col")
    l = lax.axis_index("leaf")
    x = lax.div(c, 2)
    core = lax.rem(c, 2)
    ct = lax.div(z, 2)
    taken = [0]

    def sem():
        taken[0] += 1
        return sems.at[taken[0] - 1]

    def zed(d):
        return lax.rem(z + (d + 32), 16)

    def plane(d):
        return lax.rem(l + (d + 8), 4)

    def colm(dx, dc):
        return lax.rem(x + (dx + 4), 4) * 2 + lax.rem(core + dc, 2)

    def await_bytes(ref, s):
        pltpu.make_async_copy(ref, ref, s).wait()

    gone = sem()
    units = [0, 0]

    def size(ref):
        total = 1
        for n in ref.shape:
            total *= n
        return total // 4096

    def send(src, dst, recv_sem, where):
        units[0] += size(src)
        pltpu.make_async_remote_copy(
            src_ref=src, dst_ref=dst, send_sem=gone, recv_sem=recv_sem, device_id=where, device_id_type=MESH
        ).start()

    def send_unless(me, src, dst, recv_sem, where):
        unused = spare.at[units[1]]
        units[1] += 1

        @pl.when(me)
        def _():
            if dst is not None:
                pltpu.make_async_copy(src, dst, recv_sem).start()
            pltpu.make_async_copy(src, unused, gone).start()

        @pl.when(jnp.logical_not(me))
        def _():
            send(src, where[0], recv_sem, where[1])

    def load(pairs):
        s, total = sem(), 0
        for src, dst in pairs:
            pltpu.make_async_copy(src, dst, s).start()
            total += size(dst) * (2 if dst.dtype == F32 else 1)
        return lambda: await_bytes(bytes_of.at[pl.ds(0, total)], s)

    def halves(src, dst):
        return [(src.at[:, pl.ds(256 * b, 256)], dst.at[b]) for b in range(2)]

    barrier = pltpu.get_barrier_semaphore()

    def greet(where):
        pl.semaphore_signal(barrier, inc=1, device_id=where, device_id_type=MESH)

    greeted = 0
    for b in range(2):
        for k in range(8):
            greet((2 * c + b, k, l))
            greeted += 1
    for dy in range(4):
        for dx, dc in NEAR + [(0, 0)]:
            if (dy, dx, dc) != (0, 0, 0):
                greet((z, colm(dx, dc), plane(dy)))
                greeted += 1
    for d in (-2, -1, 1, 2):
        greet((zed(d), c, l))
        greeted += 1

    first_load = load([(leaf_rhs.at[0], b_leaf), (leaf_lower_inv.at[0], i_ll)])
    load_ll = load(halves(leaf_lower.at[0, 0], w_ll))
    pairs = [(root_rhs, b_root), (root_lower_inv, i_rl), (leaf_upper_inv.at[0], i_lu), (root_upper_inv, i_ru)]
    for m in range(2):
        for j in range(2):
            pairs += halves(coupling_lower.at[0, m, j], w_cl.at[m, j])
            pairs += halves(coupling_upper.at[0, m, j], w_cu.at[m, j])
    pairs += halves(root_lower.at[0], w_rl)
    pairs += halves(leaf_upper.at[0, 0], w_lu)
    pairs += halves(root_upper.at[0], w_ru)
    load_rest = load(pairs)

    p_y[...] = jnp.zeros_like(p_y)
    p_a[...] = jnp.zeros_like(p_a)
    p_w[...] = jnp.zeros_like(p_w)

    def spread_far(src, v):
        r = sem()
        kind = 2 * lax.rem(z, 2) + lax.div(c, 4)
        off = lax.rem(kind - z + 16, 4)
        dst = v.at[lax.rem(z, 2), c]
        for i in (2, 1, 3):
            send(src, dst, r, (zed(off + 4 * i), ct, l))
        first = zed(off)
        me = (first == z) & (ct == c)
        send_unless(me, src, dst, r, (dst, (first, ct, l)))
        return lambda: await_bytes(v.at[0, pl.ds(0, 4)], r)

    def class_of(d):
        j = lax.rem(z + (d + 16), 4)
        return lax.div(j, 2), lax.rem(j, 2) * 4

    def spread_near(v):
        b, first = class_of(0)
        block = v.at[b, pl.ds(first, 4)]
        parts = [v.at[b, pl.ds(first, 2)], v.at[b, pl.ds(first + 2, 2)]]
        r_next, r_prev, r_far = sem(), sem(), sem()
        send(block, block, r_next, (zed(1), c, l))
        send(block, block, r_prev, (zed(-1), c, l))
        send(parts[0], parts[0], r_far, (zed(2), c, l))
        send(parts[1], parts[1], r_far, (zed(-2), c, l))

        def arrivals():
            for d, r in ((-1, r_next), (1, r_prev), (2, r_far)):
                await_bytes(block, r)
                yield d

        return arrivals

    def add_class(acc, v, w, d):
        b, first = class_of(d)
        rows = v[b, pl.ds(first, 4)].reshape(4 * R, 256)
        acc[pl.ds(first, 4)] += dot_t(rows, w[b]).reshape(4, R, 256)

    def add_all(acc, v, w):
        total = dot_t(v[0].reshape(8 * R, 256), w[0]) + dot_t(v[1].reshape(8 * R, 256), w[1])
        acc[...] += total.reshape(8, R, 256)

    def reduce_start(p, s_ref, r_ref):
        r = sem()
        s_ref[...] = p[...].astype(BF)
        for i, (dx, dc) in enumerate(NEAR):
            other = colm(dx, dc)
            send(s_ref.at[other], r_ref.at[i], r, (z, other, l))

        def result():
            await_bytes(r_ref, r)
            total = p[c]
            for i in range(7):
                total = total + r_ref[i].astype(F32)
            return total

        return result

    a_recv = [sem(), sem()]

    def reduce_leaf_start(m, h):
        s_ref = s_a.at[m, h]
        s_ref[...] = p_a[m, h].astype(BF)
        slot = lax.rem(l - h + 4, 4)
        for k, (dx, dc) in enumerate(NEAR + [(0, 0)]):
            other = colm(dx, dc)
            if k < 7:
                send(s_ref.at[other], r_a.at[m, 4 * k + slot], a_recv[m], (z, other, h))
            else:
                there = (r_a.at[m, 27 + slot], (z, other, h))
                send_unless(l == h, s_ref.at[other], None, a_recv[m], there)

    def reduce_leaf_result(m):
        await_bytes(r_a.at[m], a_recv[m])
        total = p_a[m, l, c]
        for slot in range(31):
            total = total + r_a[m, slot].astype(F32)
        return total

    def spread_root(src, dst):
        r = sem()
        for d in (8, 7, 9, 6, 10, 5, 11, 4, 12, 3, 13, 2, 14, 1, 15):
            send(src, dst, r, (zed(d), ct, l))
        send_unless(ct == c, src, dst, r, (dst, (z, ct, l)))
        return lambda: await_bytes(v_z, r)

    def multiply_root(get, w, p):
        total = dot_t(get(0).reshape(128, 256), w[0]) + dot_t(get(1).reshape(128, 256), w[1])
        p[...] = total.reshape(8, 16, 256)

    lower_b = lambda k, h: b_leaf[k, pl.ds(R * h, R)].astype(F32)

    pl.semaphore_wait(barrier, greeted)
    first_load()

    def lower(h):
        yb[0, h] = solve(i_ll.at[0], lower_b(0, h))
        far = spread_far(yb.at[0, h], v_y.at[0, h])
        if h == 0:
            load_ll()
        yield
        far()
        near = spread_near(v_y.at[0, h])
        add_class(p_y.at[h], v_y.at[0, h], w_ll, 0)
        yield
        for d in near():
            add_class(p_y.at[h], v_y.at[0, h], w_ll, d)
        total = reduce_start(p_y.at[h], s_y.at[h], r_y.at[h])
        if h == 0:
            load_rest()
        for m in range(2):
            add_all(p_a.at[m, h], v_y.at[0, h], w_cl.at[m, 0])
        yield
        yb[1, h] = solve(i_ll.at[1], lower_b(1, h) - total())
        far = spread_far(yb.at[1, h], v_y.at[1, h])
        yield
        far()
        near = spread_near(v_y.at[1, h])
        add_class(p_a.at[0, h], v_y.at[1, h], w_cl.at[0, 1], 0)
        yield
        for d in near():
            add_class(p_a.at[0, h], v_y.at[1, h], w_cl.at[0, 1], d)
        reduce_leaf_start(0, h)
        yield
        add_all(p_a.at[1, h], v_y.at[1, h], w_cl.at[1, 1])
        reduce_leaf_start(1, h)

    gathered = {}

    def gather_send(m):
        gathered[m] = [None] + [sem() for _ in range(3)]
        for d in (2, 1, 3):
            send(v_x.at[m, l], v_x.at[m, l], gathered[m][4 - d], (z, c, plane(d)))

    def gather_wait(m, t):
        if t:
            await_bytes(v_z, gathered[m][t])

    ro_recv = sem()

    def out_send(m):
        ro[m, l] = xb[m]
        for d in (2, 1, 3):
            send(xb.at[m], ro.at[m, l], ro_recv, (z, c, plane(d)))

    def root():
        rows = pl.ds(pl.multiple_of(l * 16, 16), 16)
        zb[0] = solve(i_rl.at[0], b_root[0, rows].astype(F32) - reduce_leaf_result(0))
        done = spread_root(zb.at[0], v_z.at[lax.rem(z, 2), c])
        base1[...] = b_root[1, rows].astype(F32) - reduce_leaf_result(1)
        done()
        multiply_root(lambda b: v_z[b], w_rl, p_r.at[0])
        total = reduce_start(p_r.at[0], s_r.at[0], r_r.at[0])
        z1 = solve(i_rl.at[1], base1[...] - total())
        xb[1] = solve(i_ru.at[1], z1.astype(F32))
        done = spread_root(xb.at[1], v_x.at[1, l, lax.rem(z, 2), c])
        out_send(1)
        done()
        gather_send(1)
        multiply_root(lambda b: v_x[1, l, b], w_ru, p_r.at[1])
        total = reduce_start(p_r.at[1], s_r.at[1], r_r.at[1])
        xb[0] = solve(i_ru.at[0], zb[0].astype(F32) - total())
        done = spread_root(xb.at[0], v_x.at[0, l, lax.rem(z, 2), c])
        out_send(0)
        for t in TURNS:
            gather_wait(1, t)
            for k in (1, 0):
                add_all(p_w.at[k, t], v_x.at[1, plane(t)], w_cu.at[k, 1])
        done()
        gather_send(0)

    def upper(t):
        h = plane(t)
        rows = pl.ds(pl.multiple_of(h * R, R), R)
        gather_wait(0, t)
        add_all(p_w.at[1, t], v_x.at[0, h], w_cu.at[1, 0])
        total = reduce_start(p_w.at[1, t], s_w.at[1, t], r_w.at[1, t])
        add_all(p_w.at[0, t], v_x.at[0, h], w_cu.at[0, 0])
        yield
        wb[t] = solve(i_lu.at[1], yb[1, h].astype(F32) - total())
        far = spread_far(wb.at[t], v_w.at[t])
        leaf_out[0, 1, rows] = wb[t]
        yield
        far()
        near = spread_near(v_w.at[t])
        add_class(p_w.at[0, t], v_w.at[t], w_lu, 0)
        yield
        for d in near():
            add_class(p_w.at[0, t], v_w.at[t], w_lu, d)
        total = reduce_start(p_w.at[0, t], s_w.at[0, t], r_w.at[0, t])
        yield
        leaf_out[0, 0, rows] = solve(i_lu.at[0], yb[0, h].astype(F32) - total())

    def in_turn(chains):
        chains = list(chains)
        while chains:
            chains = [chain for chain in chains if next(chain, chain) is not chain]

    in_turn([lower(h) for h in range(H)])
    root()
    chains = [upper(t) for t in range(4)]
    for t in ORDER:
        next(chains[t], None)
    await_bytes(bytes_of.at[pl.ds(0, 6)], ro_recv)
    for m in range(2):
        root_out[m] = ro[m].reshape(64, 256)
    await_bytes(bytes_of.at[pl.ds(0, units[0])], gone)


def on_device(*args):
    vmem = pltpu.VMEM
    scratch = [
        vmem((2, 64, 256), BF),
        vmem((2, 64, 256), BF),
        vmem((2, 256, 256), BF),
        vmem((2, 2, 2, 256, 256), BF),
        vmem((2, 256, 256), BF),
        vmem((2, 256, 256), BF),
        vmem((2, 2, 2, 256, 256), BF),
        vmem((2, 256, 256), BF),
        vmem((2, 2, 128, 128), F32),
        vmem((2, 2, 128, 128), F32),
        vmem((2, 2, 128, 128), F32),
        vmem((2, 2, 128, 128), F32),
        vmem((2, H, R, 256), BF),
        vmem((H, R, 256), BF),
        vmem((2, 16, 256), BF),
        vmem((2, 16, 256), BF),
        vmem((16, 256), F32),
        vmem((2, H, 2, 8, R, 256), BF),
        vmem((H, 2, 8, R, 256), BF),
        vmem((2, 8, 16, 256), BF),
        vmem((2, H, 2, 8, R, 256), BF),
        vmem((H, 8, R, 256), F32),
        vmem((2, H, 8, R, 256), F32),
        vmem((2, H, 8, R, 256), F32),
        vmem((2, 8, 16, 256), F32),
        vmem((H, 8, R, 256), BF),
        vmem((2, H, 8, R, 256), BF),
        vmem((2, H, 8, R, 256), BF),
        vmem((2, 8, 16, 256), BF),
        vmem((H, 7, R, 256), BF),
        vmem((2, 31, 16, 256), BF),
        vmem((2, H, 7, R, 256), BF),
        vmem((2, 7, 16, 256), BF),
        vmem((2, 4, 16, 256), BF),
        vmem((24, 16, 256), BF),
        vmem((1024, 16, 256), BF),
        pltpu.SemaphoreType.DMA((N_SEM,)),
    ]
    return pl.pallas_call(
        kernel,
        out_shape=(
            jax.ShapeDtypeStruct((1, 2, 64, 256), BF),
            jax.ShapeDtypeStruct((2, 64, 256), BF),
        ),
        in_specs=[pl.BlockSpec(memory_space=pl.ANY)] * 12,
        out_specs=(pl.BlockSpec(memory_space=pltpu.VMEM),) * 2,
        scratch_shapes=scratch,
        compiler_params=pltpu.CompilerParams(
            collective_id=0, has_side_effects=True, vmem_limit_bytes=63 * 2**20
        ),
    )(*args)


def solution(mesh):
    placed = (
        P("leaf", None, "col", "row"),
        P(None, "col", "row"),
        P("leaf", None, "row", "col"),
        P("leaf", None, None, "row", "col"),
        P(None, "row", "col"),
        P("leaf", None, "row", "col"),
        P("leaf", None, None, "row", "col"),
        P(None, "row", "col"),
        P("leaf", None, "row", None, None),
        P(None, "row", None, None),
        P("leaf", None, "row", None, None),
        P(None, "row", None, None),
    )
    return jax.shard_map(
        on_device,
        mesh=mesh,
        in_specs=placed,
        out_specs=(P("leaf", None, "col", "row"), P(None, "col", "row")),
        check_vma=False,
    )
```

time: 150 us -> 133 us (0.89)
  local copies, waits for them, and re-layouts: 13 us -> 2.14 us
  Pallas kernels: 136 us -> 129 us
    unnamed x26 -> x4, local copies, waits for them, and re-layouts: 13 us -> 2.14 us
    pallas_call x1, Pallas kernels: 136 us -> 129 us  [on_device(): pl.pallas_call(kernel, out_shape=(jax.ShapeDtypeStruct((1, 2, 64, 256), B...]
where the time goes in v2:
time: 133 us; the launch traced here: 132 us
  Pallas kernels  129 us (97%)
  local copies, waits for them, and re-layouts  2.14 us (2%)
    pallas_call x1, Pallas kernels, on_device(): pl.pallas_call(kernel, out_shape=(jax.ShapeDtypeStruct((1, 2, 64, 256), B...  129 us

profile of v2, /device:TPU:1, one launch (start us, length us, event | category | flops | bytes accessed | tf_op | source)
XLA Modules:
  0.0 131.6 jit_solution(15945640298285519059)
XLA Ops:
  0.6 128.8 %shard_map.131 = (bf16[1,2,64,256]{3,2,1,0:T(8,128)(2,1)}, bf16[2,64,256]{2,1,0:T(8,128)(2,1)}) custom-call(bf16[1,2,64,256]{3,2,1,0:T(8,128)(2,1)} %leaf_rhs.1, bf16[2,64,256]{2,1,0:T(8,128)(2,1)} %root_rhs.1, bf16[1,1,256,512]{3,2,1,0:T(8,128)(2,1)} %leaf_lower.1, bf16[1,2,2,256,512]{4,3,2,1,0:T(8,128)(2,1)} %coupling_lower.1, ...), custom_call_target="tpu_custom_call" | custom-call | tf_op jit(solution)/shard_map/pallas_call | solution.py:439
  129.5 0.0 copy-start
  129.5 1.5 %copy.16 = bf16[1,2,64,256]{3,2,1,0:T(8,128)(2,1)} copy(bf16[1,2,64,256]{3,2,1,0:T(8,128)(2,1)} %get-tuple-element.4) | data formatting | bytes 131072
  131.0 0.0 copy-done
  131.0 0.6 copy.17
Async XLA Ops:
  129.5 1.5 %copy-start = (bf16[2,64,256]{2,1,0:T(8,128)(2,1)S(1)}, bf16[2,64,256]{2,1,0:T(8,128)(2,1)}, u32[]{:S(2)}) copy-start(bf16[2,64,256]{2,1,0:T(8,128)(2,1)} %get-tuple-element.5) | copy-start | bytes 196612

commit v3 on v2

--- a/solution.py
+++ b/solution.py
@@ -8,12 +8,12 @@
 MESH = pl.DeviceIdType.MESH
 H = 4
 TURNS = (0, 1, 3, 2)
-ORDER = (0, 0, 1, 3, 2, 0, 1, 3, 2, 0, 1, 3, 2, 0, 1, 3, 2, 1, 3, 2)
+ORDER = (0, 0, 0, 1, 3, 2, 1, 3, 2, 0, 1, 3, 2, 0, 1, 3, 2, 0, 1, 3, 2, 1, 3, 2)
 R = 64 // H
 BF = jnp.bfloat16
 F32 = jnp.float32
 NEAR = [(2, 0), (2, 1), (1, 0), (1, 1), (3, 0), (3, 1), (0, 1)]
-N_SEM = 88
+N_SEM = 54
 
 
 def dot_t(a, b):
@@ -86,6 +86,7 @@
     ro,
     spare,
     bytes_of,
+    i_both,
     sems,
 ):
     z = lax.axis_index("row")
@@ -188,41 +189,23 @@
 
     def spread_far(src, v):
         r = sem()
-        kind = 2 * lax.rem(z, 2) + lax.div(c, 4)
-        off = lax.rem(kind - z + 16, 4)
+        off = 1 + lax.rem(z, 2) + lax.div(c, 4)
         dst = v.at[lax.rem(z, 2), c]
-        for i in (2, 1, 3):
+        for i in (2, 1, 3, 0):
             send(src, dst, r, (zed(off + 4 * i), ct, l))
-        first = zed(off)
-        me = (first == z) & (ct == c)
-        send_unless(me, src, dst, r, (dst, (first, ct, l)))
         return lambda: await_bytes(v.at[0, pl.ds(0, 4)], r)
 
-    def class_of(d):
-        j = lax.rem(z + (d + 16), 4)
-        return lax.div(j, 2), lax.rem(j, 2) * 4
-
     def spread_near(v):
-        b, first = class_of(0)
+        j = lax.rem(z - 2 * c + 31, 4)
+        b, first = lax.div(j, 2), lax.rem(j, 2) * 4
         block = v.at[b, pl.ds(first, 4)]
         parts = [v.at[b, pl.ds(first, 2)], v.at[b, pl.ds(first + 2, 2)]]
-        r_next, r_prev, r_far = sem(), sem(), sem()
-        send(block, block, r_next, (zed(1), c, l))
-        send(block, block, r_prev, (zed(-1), c, l))
-        send(parts[0], parts[0], r_far, (zed(2), c, l))
-        send(parts[1], parts[1], r_far, (zed(-2), c, l))
-
-        def arrivals():
-            for d, r in ((-1, r_next), (1, r_prev), (2, r_far)):
-                await_bytes(block, r)
-                yield d
-
-        return arrivals
-
-    def add_class(acc, v, w, d):
-        b, first = class_of(d)
-        rows = v[b, pl.ds(first, 4)].reshape(4 * R, 256)
-        acc[pl.ds(first, 4)] += dot_t(rows, w[b]).reshape(4, R, 256)
+        r = sem()
+        send(parts[0], parts[0], r, (zed(2), c, l))
+        send(parts[1], parts[1], r, (zed(-2), c, l))
+        send(block, block, r, (zed(1), c, l))
+        send(block, block, r, (zed(-1), c, l))
+        return lambda: await_bytes(v.at[:, pl.ds(0, 6)], r)
 
     def add_all(acc, v, w):
         total = dot_t(v[0].reshape(8 * R, 256), w[0]) + dot_t(v[1].reshape(8 * R, 256), w[1])
@@ -278,24 +261,32 @@
 
     lower_b = lambda k, h: b_leaf[k, pl.ds(R * h, R)].astype(F32)
 
+    first_load()
+    for h in range(H):
+        yb[0, h] = solve(i_ll.at[0], lower_b(0, h))
+    load_rest()
+    for g in range(2):
+        i_both[g] = lax.dot_general(
+            i_ru[1, g],
+            i_rl[1, g],
+            (((1,), (0,)), ((), ())),
+            preferred_element_type=F32,
+            precision=lax.Precision.HIGHEST,
+        )
     pl.semaphore_wait(barrier, greeted)
-    first_load()
 
     def lower(h):
-        yb[0, h] = solve(i_ll.at[0], lower_b(0, h))
         far = spread_far(yb.at[0, h], v_y.at[0, h])
+        yield
+        far()
+        near = spread_near(v_y.at[0, h])
+        yield
         if h == 0:
             load_ll()
-        yield
-        far()
-        near = spread_near(v_y.at[0, h])
-        add_class(p_y.at[h], v_y.at[0, h], w_ll, 0)
-        yield
-        for d in near():
-            add_class(p_y.at[h], v_y.at[0, h], w_ll, d)
+        near()
+        add_all(p_y.at[h], v_y.at[0, h], w_ll)
         total = reduce_start(p_y.at[h], s_y.at[h], r_y.at[h])
-        if h == 0:
-            load_rest()
+        yield
         for m in range(2):
             add_all(p_a.at[m, h], v_y.at[0, h], w_cl.at[m, 0])
         yield
@@ -304,14 +295,10 @@
         yield
         far()
         near = spread_near(v_y.at[1, h])
-        add_class(p_a.at[0, h], v_y.at[1, h], w_cl.at[0, 1], 0)
-        yield
-        for d in near():
-            add_class(p_a.at[0, h], v_y.at[1, h], w_cl.at[0, 1], d)
+        yield
+        near()
+        add_all(p_a.at[0, h], v_y.at[1, h], w_cl.at[0, 1])
         reduce_leaf_start(0, h)
-        yield
-        add_all(p_a.at[1, h], v_y.at[1, h], w_cl.at[1, 1])
-        reduce_leaf_start(1, h)
 
     gathered = {}
 
@@ -335,12 +322,14 @@
         rows = pl.ds(pl.multiple_of(l * 16, 16), 16)
         zb[0] = solve(i_rl.at[0], b_root[0, rows].astype(F32) - reduce_leaf_result(0))
         done = spread_root(zb.at[0], v_z.at[lax.rem(z, 2), c])
+        for h in range(H):
+            add_all(p_a.at[1, h], v_y.at[1, h], w_cl.at[1, 1])
+            reduce_leaf_start(1, h)
         base1[...] = b_root[1, rows].astype(F32) - reduce_leaf_result(1)
         done()
         multiply_root(lambda b: v_z[b], w_rl, p_r.at[0])
         total = reduce_start(p_r.at[0], s_r.at[0], r_r.at[0])
-        z1 = solve(i_rl.at[1], base1[...] - total())
-        xb[1] = solve(i_ru.at[1], z1.astype(F32))
+        xb[1] = solve(i_both, base1[...] - total())
         done = spread_root(xb.at[1], v_x.at[1, l, lax.rem(z, 2), c])
         out_send(1)
         done()
@@ -363,6 +352,7 @@
         gather_wait(0, t)
         add_all(p_w.at[1, t], v_x.at[0, h], w_cu.at[1, 0])
         total = reduce_start(p_w.at[1, t], s_w.at[1, t], r_w.at[1, t])
+        yield
         add_all(p_w.at[0, t], v_x.at[0, h], w_cu.at[0, 0])
         yield
         wb[t] = solve(i_lu.at[1], yb[1, h].astype(F32) - total())
@@ -371,10 +361,9 @@
         yield
         far()
         near = spread_near(v_w.at[t])
-        add_class(p_w.at[0, t], v_w.at[t], w_lu, 0)
-        yield
-        for d in near():
-            add_class(p_w.at[0, t], v_w.at[t], w_lu, d)
+        yield
+        near()
+        add_all(p_w.at[0, t], v_w.at[t], w_lu)
         total = reduce_start(p_w.at[0, t], s_w.at[0, t], r_w.at[0, t])
         yield
         leaf_out[0, 0, rows] = solve(i_lu.at[0], yb[0, h].astype(F32) - total())
@@ -434,6 +423,7 @@
         vmem((2, 4, 16, 256), BF),
         vmem((24, 16, 256), BF),
         vmem((1024, 16, 256), BF),
+        vmem((2, 128, 128), F32),
         pltpu.SemaphoreType.DMA((N_SEM,)),
     ]
     return pl.pallas_call(

time: 133 us -> 129 us (0.970)
  Pallas kernels: 129 us -> 126 us
    pallas_call x1, Pallas kernels: 129 us -> 126 us  [on_device(): pl.pallas_call(kernel, out_shape=(jax.ShapeDtypeStruct((1, 2, 64, 256), B...]
where the time goes in v3:
time: 129 us; the launch traced here: 128 us
  Pallas kernels  126 us (98%)
  local copies, waits for them, and re-layouts  2.14 us (2%)
    pallas_call x1, Pallas kernels, on_device(): pl.pallas_call(kernel, out_shape=(jax.ShapeDtypeStruct((1, 2, 64, 256), B...  126 us

profile of v3, /device:TPU:1, one launch (start us, length us, event | category | flops | bytes accessed | tf_op | source)
XLA Modules:
  0.0 128.4 jit_solution(3372177300608963165)
XLA Ops:
  0.6 125.6 %shard_map.131 = (bf16[1,2,64,256]{3,2,1,0:T(8,128)(2,1)}, bf16[2,64,256]{2,1,0:T(8,128)(2,1)}) custom-call(bf16[1,2,64,256]{3,2,1,0:T(8,128)(2,1)} %leaf_rhs.1, bf16[2,64,256]{2,1,0:T(8,128)(2,1)} %root_rhs.1, bf16[1,1,256,512]{3,2,1,0:T(8,128)(2,1)} %leaf_lower.1, bf16[1,2,2,256,512]{4,3,2,1,0:T(8,128)(2,1)} %coupling_lower.1, ...), custom_call_target="tpu_custom_call" | custom-call | tf_op jit(solution)/shard_map/pallas_call | solution.py:429
  126.2 0.0 copy-start
  126.3 1.5 %copy.16 = bf16[1,2,64,256]{3,2,1,0:T(8,128)(2,1)} copy(bf16[1,2,64,256]{3,2,1,0:T(8,128)(2,1)} %get-tuple-element.4) | data formatting | bytes 131072
  127.8 0.0 copy-done
  127.8 0.6 copy.17
Async XLA Ops:
  126.2 1.5 %copy-start = (bf16[2,64,256]{2,1,0:T(8,128)(2,1)S(1)}, bf16[2,64,256]{2,1,0:T(8,128)(2,1)}, u32[]{:S(2)}) copy-start(bf16[2,64,256]{2,1,0:T(8,128)(2,1)} %get-tuple-element.5) | copy-start | bytes 196612

commit v4 on v3

--- a/solution.py
+++ b/solution.py
@@ -13,7 +13,7 @@
 BF = jnp.bfloat16
 F32 = jnp.float32
 NEAR = [(2, 0), (2, 1), (1, 0), (1, 1), (3, 0), (3, 1), (0, 1)]
-N_SEM = 54
+N_SEM = 57
 
 
 def dot_t(a, b):
@@ -249,11 +249,13 @@
         return total
 
     def spread_root(src, dst):
-        r = sem()
+        first = taken[0]
+        taken[0] += 2
+        r = sems.at[first + lax.rem(z, 2)]
         for d in (8, 7, 9, 6, 10, 5, 11, 4, 12, 3, 13, 2, 14, 1, 15):
             send(src, dst, r, (zed(d), ct, l))
         send_unless(ct == c, src, dst, r, (dst, (z, ct, l)))
-        return lambda: await_bytes(v_z, r)
+        return lambda b: await_bytes(v_z.at[0], sems.at[first + b])
 
     def multiply_root(get, w, p):
         total = dot_t(get(0).reshape(128, 256), w[0]) + dot_t(get(1).reshape(128, 256), w[1])
@@ -302,10 +304,15 @@
 
     gathered = {}
 
-    def gather_send(m):
+    close = (lax.rem(z - 2 * c + 31, 16) < 8).astype(jnp.int32)
+
+    def gather_send(m, done):
         gathered[m] = [None] + [sem() for _ in range(3)]
-        for d in (2, 1, 3):
-            send(v_x.at[m, l], v_x.at[m, l], gathered[m][4 - d], (z, c, plane(d)))
+        for b in (close, 1 - close):
+            done(b)
+            part = v_x.at[m, l, b]
+            for d in (2, 1, 3):
+                send(part, part, gathered[m][4 - d], (z, c, plane(d)))
 
     def gather_wait(m, t):
         if t:
@@ -326,14 +333,14 @@
             add_all(p_a.at[1, h], v_y.at[1, h], w_cl.at[1, 1])
             reduce_leaf_start(1, h)
         base1[...] = b_root[1, rows].astype(F32) - reduce_leaf_result(1)
-        done()
+        done(0)
+        done(1)
         multiply_root(lambda b: v_z[b], w_rl, p_r.at[0])
         total = reduce_start(p_r.at[0], s_r.at[0], r_r.at[0])
         xb[1] = solve(i_both, base1[...] - total())
         done = spread_root(xb.at[1], v_x.at[1, l, lax.rem(z, 2), c])
         out_send(1)
-        done()
-        gather_send(1)
+        gather_send(1, done)
         multiply_root(lambda b: v_x[1, l, b], w_ru, p_r.at[1])
         total = reduce_start(p_r.at[1], s_r.at[1], r_r.at[1])
         xb[0] = solve(i_ru.at[0], zb[0].astype(F32) - total())
@@ -343,8 +350,7 @@
             gather_wait(1, t)
             for k in (1, 0):
                 add_all(p_w.at[k, t], v_x.at[1, plane(t)], w_cu.at[k, 1])
-        done()
-        gather_send(0)
+        gather_send(0, done)
 
     def upper(t):
         h = plane(t)

time: 129 us -> 129 us (level)
  no operation moved by 1% of the time
where the time goes in v4:
time: 129 us
  Pallas kernels  126 us (98%)
  local copies, waits for them, and re-layouts  2.14 us (2%)
    pallas_call x1, Pallas kernels, on_device(): pl.pallas_call(kernel, out_shape=(jax.ShapeDtypeStruct((1, 2, 64, 256), B...  126 us

profile of v4, /device:TPU:1, one launch (start us, length us, event | category | flops | bytes accessed | tf_op | source)
XLA Modules:
  0.0 129.2 jit_solution(8505188856901317460)
XLA Ops:
  0.6 126.4 %shard_map.131 = (bf16[1,2,64,256]{3,2,1,0:T(8,128)(2,1)}, bf16[2,64,256]{2,1,0:T(8,128)(2,1)}) custom-call(bf16[1,2,64,256]{3,2,1,0:T(8,128)(2,1)} %leaf_rhs.1, bf16[2,64,256]{2,1,0:T(8,128)(2,1)} %root_rhs.1, bf16[1,1,256,512]{3,2,1,0:T(8,128)(2,1)} %leaf_lower.1, bf16[1,2,2,256,512]{4,3,2,1,0:T(8,128)(2,1)} %coupling_lower.1, ...), custom_call_target="tpu_custom_call" | custom-call | tf_op jit(solution)/shard_map/pallas_call | solution.py:435
  127.0 0.0 copy-start
  127.0 1.5 %copy.16 = bf16[1,2,64,256]{3,2,1,0:T(8,128)(2,1)} copy(bf16[1,2,64,256]{3,2,1,0:T(8,128)(2,1)} %get-tuple-element.4) | data formatting | bytes 131072
  128.5 0.0 copy-done
  128.5 0.6 copy.17
Async XLA Ops:
  127.0 1.5 %copy-start = (bf16[2,64,256]{2,1,0:T(8,128)(2,1)S(1)}, bf16[2,64,256]{2,1,0:T(8,128)(2,1)}, u32[]{:S(2)}) copy-start(bf16[2,64,256]{2,1,0:T(8,128)(2,1)} %get-tuple-element.5) | copy-start | bytes 196612
